TPU v7x, 256 devices: a whole 4x4x8 slice. The times are simulated.
256 devices in a mesh: eig: 16 (over x, z_hi, core), store: 16 (over z_lo, y).
Axes of the slice: x: 4, y: 4, z: 8 (z_hi: 2, z_lo: 4; z = z_hi * 4 + z_lo), core: 2. Of those that a mesh axis runs over, the one named last changes fastest.
Arguments:
- acts: bfloat16 [2048, 8192], P('store'), may hold values from -6 to 6
- basis: bfloat16 [8192, 8192], P('store', 'eig'), may hold values from -0.0625 to 0.0625
- eigvals: float32 [64, 8192], P(None, 'eig'), may hold values from 0.5 to 8
- projection: bfloat16 [8192, 64], P('eig'), may hold values from -0.0625 to 0.0625
- out_factor: float32 [2048, 64], P('store', 'eig'), may hold values from -6 to 6
- store: bfloat16 [32768, 4096], P('store', 'eig'), may hold values from -0.09375 to 0.09375
Outputs:
- scores: float32 [2048, 32768], P(None, ('store', 'eig'))
All inputs are finite; a program needn't handle non-finite values.
Results may differ from a plain program's by a relative error of at most 0.0041.
Values may be sent and summed in bfloat16 or wider, within the bound.
A program may use at most 64 MiB of HBM per device.

v0:
```python
import jax
import jax.numpy as jnp
from jax import lax
from jax.sharding import PartitionSpec as P

K_OUT = 64
K_IN = 64


damping = 0.1


def joined_along(blocks, dim):
    blocks = jnp.moveaxis(blocks, 0, dim)
    shape = blocks.shape
    return blocks.reshape(*shape[:dim], shape[dim] * shape[dim + 1], *shape[dim + 2 :])


def from_everyone(shard, axis):
    copies = jnp.broadcast_to(shard, (lax.axis_size(axis), *shard.shape))
    return lax.all_to_all(copies, axis, split_axis=0, concat_axis=0, tiled=True)


def gathered_copies(shard, axis, dim):
    return joined_along(from_everyone(shard, axis), dim)


def body(acts, basis, eigvals, projection, out_factor, store):
    queries = acts.shape[0]
    columns = basis.shape[1]
    rotated = jnp.dot(
        acts, lax.all_gather(basis, "store", axis=0, tiled=True), preferred_element_type=jnp.float32
    )
    inverse = 1.0 / (eigvals + damping)
    scaled = (rotated[:, None, :] * inverse[None, :, :]).astype(jnp.bfloat16)
    partial_value = jnp.dot(
        scaled.reshape(queries * K_OUT, columns), projection, preferred_element_type=jnp.float32
    )
    partial_value = partial_value.reshape(queries, K_OUT * K_IN)
    summed = lax.psum_scatter(partial_value, "eig", scatter_dimension=1, tiled=True)
    kept = out_factor.shape[1]
    features = (summed.reshape(queries, kept, K_IN) * out_factor[:, :, None]).reshape(
        queries, kept * K_IN
    )
    features = features.astype(jnp.bfloat16)
    partial_scores = jnp.einsum(
        "qf,rf->qr",
        gathered_copies(features, "store", 0),
        store,
        preferred_element_type=jnp.float32,
    )
    return lax.psum_scatter(partial_scores, "eig", scatter_dimension=1, tiled=True)


def solution(mesh):
    placed = (
        P("store", None),
        P("store", "eig"),
        P(None, "eig"),
        P("eig", None),
        P("store", "eig"),
        P("store", "eig"),
    )
    return jax.shard_map(
        body, mesh=mesh, in_specs=placed, out_specs=P(None, ("store", "eig")), check_vma=False
    )
```

profile of v0, /device:TPU:1, one launch (start us, length us, event | category | flops | bytes accessed | tf_op | source)
XLA Modules:
  0.0 479.9 jit_solution(4561740160038415110)
XLA Ops:
  6.5 0.0 copy-start
  6.5 0.0 all-gather.2.cloned.1.call-start
  6.5 0.7 all-gather.2.cloned.1.call-update
  7.3 0.0 reduce-scatter.3.cloned.1.call-start
  7.3 0.9 add_divide_fusion
  8.2 107.2 %all-gather.2.cloned.1.call-done = bf16[8192,512]{1,0:T(8,128)(2,1)} async-done(((bf16[512,512]{1,0:T(8,128)(2,1)}), bf16[8192,512]{1,0:T(8,128)(2,1)}) %all-gather.2.cloned.1.call-update) | async-done | bytes 8388624 | tf_op jit(solution)/shard_map/all_gather | solution.py:32
  115.5 0.0 copy-done
  115.5 4.6 fusion
  120.1 0.0 copy-start.2
  120.1 3.4 multiply_convert_fusion
  123.5 0.0 copy-done.2
  123.5 4.3 fusion.1
  127.8 0.0 copy-start.3
  127.8 0.0 copy-start.1
  127.8 4.8 %reshape.17 = f32[128,4096]{1,0:T(8,128)} reshape(f32[8192,64]{1,0:T(8,128)} %fusion.1) | data formatting | bytes 4194304 | tf_op jit(solution)/shard_map/reshape | solution.py:39
  132.6 0.0 reduce-scatter.3.cloned.1.call-update
  132.6 0.0 reduce-scatter.5.cloned.1.call-start
  132.7 0.0 copy-done.3
  132.7 0.1 copy.9
  132.8 82.8 %reduce-scatter.3.cloned.1.call-done = f32[128,256]{1,0:T(8,128)} async-done(((f32[128,4096]{1,0:T(8,128)}), f32[128,256]{1,0:T(8,128)}) %reduce-scatter.3.cloned.1.call-update) | async-done | bytes 131088 | tf_op jit(solution)/shard_map/reduce_scatter | solution.py:40
  215.6 0.9 multiply_convert_fusion.1
  216.5 0.1 broadcast_in_dim.2
  216.6 28.1 %all_to_all.5 = bf16[16,128,256]{2,1,0:T(8,128)(2,1)S(1)} all-to-all(bf16[16,128,256]{2,1,0:T(8,128)(2,1)S(1)} %broadcast_in_dim.2), channel_id=1, replica_groups=mesh['eig'=16,'store'=16] {'store'}, dimensions={0} | all-to-all | bytes 2097152 | tf_op jit(solution)/shard_map/all_to_all | solution.py:21
  244.7 0.0 copy-done.1
  244.7 8.1 %fusion.2 = f32[2048,2048]{1,0:T(8,128)} fusion(bf16[2048,256]{1,0:T(8,128)(2,1)S(1)} %bitcast.10, bf16[2048,256]{1,0:T(8,128)(2,1)S(1)} %copy-done.1), kind=kOutput, calls=%fused_computation.5 | convolution fusion | flops 2147483648 | bytes 18874368 | tf_op jit(solution)/shard_map/qf,rf->qr/dot_general | solution.py:46
  252.8 0.0 reduce-scatter.5.cloned.1.call-update
  252.8 220.6 %reduce-scatter.5.cloned.1.call-done = f32[2048,128]{1,0:T(8,128)} async-done(((f32[2048,2048]{1,0:T(8,128)}), f32[2048,128]{1,0:T(8,128)}) %reduce-scatter.5.cloned.1.call-update) | async-done | bytes 1048592 | tf_op jit(solution)/shard_map/reduce_scatter | solution.py:52
  (1 shorter events, 0.0 us)
Async XLA Ops:
  6.5 108.9 %copy-start = (bf16[128,8192]{1,0:T(8,128)(2,1)S(1)}, bf16[128,8192]{1,0:T(8,128)(2,1)}, u32[]{:S(2)}) copy-start(bf16[128,8192]{1,0:T(8,128)(2,1)} %param.6) | copy-start | bytes 6291460
  6.5 108.9 %all-gather.2.cloned.1.call-start = ((), (), s32[]{:S(2)}) async-start(), calls=%async_computation.3 | async-start | bytes 8912896 | tf_op jit(solution)/shard_map/all_gather | solution.py:32
  7.3 208.3 %reduce-scatter.3.cloned.1.call-start = ((), (), s32[]{:S(2)}) async-start(), calls=%async_computation.4 | async-start | bytes 2228224 | tf_op jit(solution)/shard_map/reduce_scatter | solution.py:40
  120.1 3.4 copy-start.2
  127.8 4.9 %copy-start.3 = (f32[128,4]{0,1:T(4,128)S(1)}, f32[128,4]{0,1:T(4,128)}, u32[]{:S(2)}) copy-start(f32[128,4]{0,1:T(4,128)} %param.10) | copy-start | bytes 6148
  127.8 116.9 %copy-start.1 = (bf16[2048,256]{1,0:T(8,128)(2,1)S(1)}, bf16[2048,256]{1,0:T(8,128)(2,1)}, u32[]{:S(2)}) copy-start(bf16[2048,256]{1,0:T(8,128)(2,1)} %param.11) | copy-start | bytes 3145732
  132.6 340.8 %reduce-scatter.5.cloned.1.call-start = ((), (), s32[]{:S(2)}) async-start(), calls=%async_computation.5 | async-start | bytes 17825792 | tf_op jit(solution)/shard_map/reduce_scatter | solution.py:52
Sparse Core Ops, SparseCore 0:
  9.1 106.2 all-gather.1
  132.8 82.7 reduce-scatter.2
  252.9 220.4 reduce-scatter.4
where the time goes:
time: 480 us
  waiting for transfers between devices  411 us (86%)
  blocking collectives  28.1 us (6%)
  matrix products  17 us (4%)
  between operations  13.2 us (3%)
  other arithmetic  5.2 us (1%)
  local copies, waits for them, and re-layouts  5.06 us (1%)
    reduce_scatter x1, waiting for transfers between devices, body(): lax.psum_scatter(partial_scores, 'eig', scatter_dimension=1, tiled=True)  221 us
    all_gather x1, waiting for transfers between devices, body(): lax.all_gather(basis, 'store', axis=0, tiled=True)  107 us
    reduce_scatter x1, waiting for transfers between devices, body(): lax.psum_scatter(partial_value, 'eig', scatter_dimension=1, tiled=True)  82.8 us
    all_to_all x1, blocking collectives, from_everyone(): return lax.all_to_all(copies, axis, split_axis=0, concat_axis=0, tiled=True)  28.1 us
  transfers between devices with their start and end apart: 3, of which 3 were waited for; matrix products, arithmetic and copies ran while one was open for 0% of the time, Pallas kernels for 0%

commit v1 on v0

v1 whole, which is shorter than its diff:
```python
import jax
import jax.numpy as jnp
from jax import lax
from jax.experimental import pallas as pl
from jax.experimental.pallas import tpu as pltpu
from jax.sharding import PartitionSpec as P

damping = 0.1
NT = (((1,), (1,)), ((), ()))


def at(x, zh, c, zl, y):
    return {"eig": x * 4 + zh * 2 + c, "store": zl * 4 + y}


def send(src, dst, sems, index, device):
    copy = pltpu.make_async_remote_copy(
        src_ref=src,
        dst_ref=dst,
        send_sem=sems.at[(0, *index)],
        recv_sem=sems.at[(1, *index)],
        device_id=device,
        device_id_type=pl.DeviceIdType.MESH,
    )
    copy.start()
    return copy


def kernel(
    acts, basis, inverse, projection, factor, store, out,
    acts_g, basis_g, part, landed, rotated, inv_g, proj_g, fac_g, store_g,
    summed, summed_in, feats, going, coming,
    own_sem, basis_sem, az_sem, ax_sem, ac_sem, st_sem, iv_sem, pr_sem, of_sem,
    zr_sem, rc_sem, cx_sem, fz_sem, fy_sem, fc_sem, sx_sem,
):
    e, s = lax.axis_index("eig"), lax.axis_index("store")
    x, zh, c = lax.div(e, 4), lax.rem(lax.div(e, 2), 2), lax.rem(e, 2)
    zl, y = lax.div(s, 4), lax.rem(s, 4)
    z = zh * 4 + zl
    piece = x * 2 + c

    def off(value, step, extent):
        return lax.rem(value + step, extent)

    def along_x(d):
        return at(off(x, d, 4), zh, c, zl, y)

    def along_y(d):
        return at(x, zh, c, zl, off(y, d, 4))

    def along_z(d):
        to = off(z, d, 8)
        return at(x, lax.div(to, 4), c, lax.rem(to, 4), y)

    def within_line(d):
        return at(x, zh, c, off(zl, d, 4), y)

    def flipped(m):
        to_h = 1 - zh if m & 2 else zh
        to_c = 1 - c if m & 1 else c
        return at(x, to_h, to_c, zl, y)

    sibling = flipped(1)

    own = [
        pltpu.make_async_copy(basis, basis_g.at[y], own_sem.at[0]),
        pltpu.make_async_copy(acts.at[:, pl.ds(pl.multiple_of(zl * 2048, 2048), 2048)], acts_g.at[zl], own_sem.at[1]),
        pltpu.make_async_copy(inverse.at[c], inv_g.at[0], own_sem.at[2]),
        pltpu.make_async_copy(projection, proj_g.at[0], own_sem.at[3]),
        pltpu.make_async_copy(factor.at[zh], fac_g.at[zh], own_sem.at[4]),
    ]
    for d in range(4):
        own.append(pltpu.make_async_copy(store.at[off(x, d, 4), zh, c], store_g.at[0, d], own_sem.at[5 + d]))
    for copy in own:
        copy.start()

    barrier = pltpu.get_barrier_semaphore()
    partners = [along_x(d) for d in range(1, 4)] + [along_y(d) for d in range(1, 4)]
    partners += [along_z(d) for d in range(1, 8)] + [sibling, flipped(3)]
    for partner in partners:
        pl.semaphore_signal(barrier, inc=1, device_id=partner, device_id_type=pl.DeviceIdType.MESH)
    pl.semaphore_wait(barrier, len(partners))

    rows = pl.ds(pl.multiple_of(piece * 16, 16), 16)
    line = []
    for d in range(1, 4):
        to = off(zl, d, 4)
        line.append(
            send(
                acts.at[rows, pl.ds(pl.multiple_of(to * 2048, 2048), 2048)],
                acts_g.at[zl, rows],
                az_sem, (d - 1,), within_line(d),
            )
        )
    blocks = [send(basis, basis_g.at[y], basis_sem, (d - 1,), along_y(d)) for d in (1, 3, 2)]
    shared, paired = [], []
    for d in range(1, 4):
        line[d - 1].wait_recv()
        slot = acts_g.at[off(zl, 4 - d, 4), rows]
        for dx in (1, 3, 2):
            shared.append((d, dx, send(slot, slot, ax_sem, (d - 1, dx - 1), along_x(dx))))
        paired.append(send(slot, slot, ac_sem, (d - 1, 0), sibling))

    behind = []
    for m in range(1, 4):
        to_h = 1 - zh if m & 2 else zh
        to_c = 1 - c if m & 1 else c
        behind.append(send(inverse.at[to_c], inv_g.at[m], iv_sem, (m - 1,), flipped(m)))
        behind.append(send(projection, proj_g.at[m], pr_sem, (m - 1,), flipped(m)))
    behind.append(send(factor.at[1 - zh], fac_g.at[zh], of_sem, (0,), flipped(2)))
    later = []
    for m in range(1, 4):
        to_h = 1 - zh if m & 2 else zh
        to_c = 1 - c if m & 1 else c
        for d in range(4):
            later.append(send(store.at[off(x, d, 4), to_h, to_c], store_g.at[m, d], st_sem, (m - 1, d), flipped(m)))

    for d, dx, copy in shared:
        copy.wait_recv()
        theirs = pl.ds(pl.multiple_of((off(x, 4 - dx, 4) * 2 + c) * 16, 16), 16)
        slot = acts_g.at[off(zl, 4 - d, 4), theirs]
        paired.append(send(slot, slot, ac_sem, (d - 1, dx), sibling))
    for copy in own[:2]:
        copy.wait()
    for copy in paired:
        copy.wait_recv()
    for copy in blocks:
        copy.wait_recv()

    partial = []
    for d in (2, 1, 3, 0):
        to = off(zl, d, 4)
        value = jnp.dot(acts_g[to], basis_g[...].reshape(2048, 512), preferred_element_type=jnp.float32)
        part[to] = value.reshape(2, 64, 512)
        for h in range(2):
            step = (4 * h + d) % 8
            if step == 0:
                continue
            to_h = 1 - zh if h else zh
            partial.append(
                send(part.at[to, to_h], landed.at[h, d], zr_sem, (h, d), at(x, to_h, c, to, y))
            )
    landed[0, 0] = part[zl, zh]
    for copy in partial:
        copy.wait_recv()
    for h in range(2):
        total = (landed[h, 0] + landed[h, 1]) + (landed[h, 2] + landed[h, 3])
        rotated[0, h] = total
    across = send(rotated.at[0], rotated.at[1], rc_sem, (0,), sibling)

    for copy in own[2:]:
        copy.wait()
    for copy in behind:
        copy.wait_recv()
    across.wait_recv()

    lanes = lax.broadcasted_iota(jnp.int32, (128, 256), 1)
    scattered = []
    for d in (2, 1, 3, 0):
        value = jnp.zeros((512, 256), jnp.float32)
        for m in range(4):
            heights = inv_g[m, off(x, d, 4)]
            scaled = (rotated[m & 1, m >> 1][None, :, :] * heights[:, None, :]).astype(jnp.bfloat16)
            block = proj_g[m]
            value += lax.dot_general(
                scaled.reshape(512, 512), jnp.concatenate([block] * 4, axis=0), NT,
                preferred_element_type=jnp.float32,
            )
        value = value.reshape(4, 128, 256)
        picked = jnp.where(
            lanes < 128,
            jnp.where(lanes < 64, value[0], value[1]),
            jnp.where(lanes < 192, value[2], value[3]),
        )
        summed[d] = picked.reshape(2, 64, 256)
        if d:
            scattered.append(send(summed.at[d], summed_in.at[d - 1], cx_sem, (d - 1,), along_x(d)))
    for copy in scattered:
        copy.wait_recv()
    total = (summed[0] + summed_in[0]) + (summed_in[1] + summed_in[2])
    feats[c, y, z] = (total * fac_g[...]).astype(jnp.bfloat16)

    mine = feats.at[c, y, z]
    ring = [send(mine, mine, fz_sem, (d - 1,), along_z(d)) for d in (1, 7, 2, 6, 3, 5, 4)]
    for copy in ring:
        copy.wait_recv()
    mine = feats.at[c, y]
    plane = {0: send(mine, mine, fc_sem, (0,), sibling)}
    gathered = {d: send(mine, mine, fy_sem, (d - 1,), along_y(d)) for d in (1, 3, 2)}
    for copy in later:
        copy.wait_recv()

    reduced = []
    for d in (0, 1, 3, 2):
        at_y = off(y, 4 - d, 4)
        if d:
            gathered[d].wait_recv()
            theirs = feats.at[c, at_y]
            plane[d] = send(theirs, theirs, fc_sem, (d,), sibling)
        plane[d].wait_recv()

        def tile(j, carry):
            value = jnp.zeros((128, 512), jnp.float32)
            for m in range(4):
                at_c = 1 - c if m & 1 else c
                at_h = 1 - zh if m & 2 else zh
                left = feats[at_c, at_y, pl.ds(j * 2, 2), at_h].reshape(128, 256)
                value += lax.dot_general(
                    left, store_g[m].reshape(512, 256), NT, preferred_element_type=jnp.float32
                )
            for half in range(2):
                rows_of = value[half * 64 : half * 64 + 64]
                at_z = j * 2 + half
                out[lax.rem(at_z, 4), at_y, lax.div(at_z, 4)] = rows_of[:, :128]
                for k in range(1, 4):
                    going[k - 1, d, at_z] = rows_of[:, k * 128 : k * 128 + 128].astype(jnp.bfloat16)
            return carry

        lax.fori_loop(0, 4, tile, 0)
        for k in (2, 1, 3):
            reduced.append(
                send(going.at[k - 1, d], coming.at[k - 1, d], sx_sem, (k - 1, d), along_x(k))
            )
    for d in (0, 1, 3, 2):
        at_y = off(y, 4 - d, 4)
        for copy in reduced[:3]:
            copy.wait_recv()
        waited, reduced = reduced[:3], reduced[3:]

        def add(j, carry):
            at_l, at_h = lax.rem(j, 4), lax.div(j, 4)
            rest = coming[0, d, j].astype(jnp.float32) + coming[1, d, j].astype(jnp.float32)
            out[at_l, at_y, at_h] = out[at_l, at_y, at_h] + (rest + coming[2, d, j].astype(jnp.float32))
            return carry

        lax.fori_loop(0, 8, add, 0)
        for copy in waited:
            copy.wait_send()

    sent = line + blocks + [copy for _, _, copy in shared] + paired + behind + later
    sent += partial + [across] + scattered + ring + list(plane.values()) + list(gathered.values())
    for copy in sent:
        copy.wait_send()


def body(acts, basis, eigvals, projection, out_factor, store):
    bf16, f32 = jnp.bfloat16, jnp.float32
    inverse = 1.0 / (eigvals + damping)
    inverse = inverse.reshape(4, 2, 2, 4, 512).transpose(2, 0, 3, 1, 4).reshape(2, 4, 8, 512)
    factor = jnp.repeat(out_factor, 64, axis=1).reshape(2, 64, 256)
    sems = [(9,)] + [
        (2, *n)
        for n in [(3,), (3,), (3, 3), (3, 4), (3, 4), (3,), (3,), (1,), (2, 4), (1,), (3,), (7,), (3,), (4,), (3, 4)]
    ]
    vmem = pl.BlockSpec(memory_space=pltpu.VMEM)
    hbm = pl.BlockSpec(memory_space=pl.ANY)
    scores = pl.pallas_call(
        kernel,
        out_shape=jax.ShapeDtypeStruct((4, 4, 2, 64, 128), f32),
        in_specs=[hbm, hbm, vmem, vmem, vmem, hbm],
        out_specs=vmem,
        scratch_shapes=[
            pltpu.VMEM((4, 128, 2048), bf16),
            pltpu.VMEM((4, 512, 512), bf16),
            pltpu.VMEM((4, 2, 64, 512), f32),
            pltpu.VMEM((2, 4, 64, 512), f32),
            pltpu.VMEM((2, 2, 64, 512), f32),
            pltpu.VMEM((4, 4, 8, 512), f32),
            pltpu.VMEM((4, 64, 512), bf16),
            pltpu.VMEM((2, 64, 256), f32),
            pltpu.VMEM((4, 4, 128, 256), bf16),
            pltpu.VMEM((4, 2, 64, 256), f32),
            pltpu.VMEM((3, 2, 64, 256), f32),
            pltpu.VMEM((2, 4, 8, 2, 64, 256), bf16),
            pltpu.VMEM((3, 4, 8, 64, 128), bf16),
            pltpu.VMEM((3, 4, 8, 64, 128), bf16),
        ]
        + [pltpu.SemaphoreType.DMA(n) for n in sems],
        compiler_params=pltpu.CompilerParams(
            collective_id=0, has_side_effects=True, vmem_limit_bytes=50 * 1024 * 1024
        ),
        cost_estimate=pl.CostEstimate(flops=4 * 10**9, bytes_accessed=10**7, transcendentals=0),
    )(acts, basis, inverse, projection.T, factor, store.reshape(4, 2, 2, 128, 256))
    return scores.reshape(2048, 128)


def solution(mesh):
    placed = (
        P("store", None),
        P("store", "eig"),
        P(None, "eig"),
        P("eig", None),
        P("store", "eig"),
        P("store", "eig"),
    )
    return jax.shard_map(
        body, mesh=mesh, in_specs=placed, out_specs=P(None, ("store", "eig")), check_vma=False
    )
```

time: 480 us -> 158 us (0.33)
  the two profiles are of different devices: /device:TPU:1 before, /device:TPU:81 now
where the time goes in v1:
time: 158 us; the launch traced here: 157 us
  Pallas kernels  151 us (96%)
  local copies, waits for them, and re-layouts  5.5 us (3%)
    pallas_call x1, Pallas kernels, body(): pl.pallas_call(kernel, out_shape=jax.ShapeDtypeStruct((4, 4, 2, 64, 128),...  151 us
    unnamed x8, local copies, waits for them, and re-layouts  4.86 us

profile of v1, /device:TPU:81, one launch (start us, length us, event | category | flops | bytes accessed | tf_op | source)
XLA Modules:
  0.0 157.3 jit_solution(7277075444333625880)
XLA Ops:
  0.0 0.8 copy.10
  0.8 0.9 add_divide_fusion
  1.8 0.1 copy.12
  1.9 0.1 reshape.13.inverse
  2.0 0.2 broadcast_in_dim.3
  2.2 0.2 reshape_reshape.3.factor
  2.4 0.0 copy-start
  2.4 1.2 copy-done
  3.6 0.0 copy-start.1
  3.6 1.0 copy-done.1
  4.7 0.0 copy-start.2
  4.7 0.8 copy-done.2
  5.5 150.8 %shard_map.64 = f32[4,4,2,64,128]{4,3,2,1,0:T(8,128)S(1)} custom-call(bf16[128,8192]{1,0:T(8,128)(2,1)} %acts.1, bf16[512,512]{1,0:T(8,128)(2,1)S(1)} %copy-done.1, f32[2,4,8,512]{3,2,1,0:T(8,128)S(1)} %reshape.13.inverse, bf16[64,512]{1,0:T(8,128)(2,1)S(1)} %bitcast.8, f32[2,64,256]{2,1,0:T(8,128)S(1)} %reshape_reshape.3.factor, ...), custom_call_target="tpu_custom_call" | custom-call | flops 4000000000 | bytes 10000000 | tf_op jit(solution)/shard_map/pallas_call | solution.py:257
  156.3 1.0 copy.14
  (1 shorter events, 0.0 us)
Async XLA Ops:
  2.4 1.2 copy-start
  3.6 1.0 copy-start.1
  4.7 0.8 copy-start.2

commit v2 on v0

v2 whole, which is shorter than its diff:
```python
import jax
import jax.numpy as jnp
from jax import lax
from jax.experimental import pallas as pl
from jax.experimental.pallas import tpu as pltpu
from jax.sharding import PartitionSpec as P

damping = 0.1
NT = (((1,), (1,)), ((), ()))


def at(x, zh, c, zl, y):
    return {"eig": x * 4 + zh * 2 + c, "store": zl * 4 + y}


LEVELS = ((0,), (1, 2), (3, 4), (5, 6), (7,))
OFFSETS = (0, 1, 7, 2, 6, 3, 5, 4)


def kernel(
    acts, basis, eigvals, projection, factor, store, out,
    acts_g, basis_g, part, landed, rotated, inv_own, inv_g, proj_g, wide, fac_g, store_g,
    summed, summed_in, feats, going, coming,
    own_sem, basis_sem, az_sem, ax_sem, ac_sem, st_sem, iv_sem, pr_sem, of_sem,
    zr_sem, rc_sem, cx_sem, fz_sem, fy_sem, fc_sem, sx_sem,
):
    e, s = lax.axis_index("eig"), lax.axis_index("store")
    x, zh, c = lax.div(e, 4), lax.rem(lax.div(e, 2), 2), lax.rem(e, 2)
    zl, y = lax.div(s, 4), lax.rem(s, 4)
    z = zh * 4 + zl
    f32, bf16 = jnp.float32, jnp.bfloat16
    sent = []

    def send(src, dst, sems, index, device):
        copy = pltpu.make_async_remote_copy(
            src_ref=src,
            dst_ref=dst,
            send_sem=sems.at[(0, *index)],
            recv_sem=sems.at[(1, *index)],
            device_id=device,
            device_id_type=pl.DeviceIdType.MESH,
        )
        copy.start()
        sent.append(copy)
        return copy

    def off(value, step, extent):
        return lax.rem(value + step, extent)

    def along_x(d):
        return at(off(x, d, 4), zh, c, zl, y)

    def along_y(d):
        return at(x, zh, c, zl, off(y, d, 4))

    def along_z(d):
        to = off(z, d, 8)
        return at(x, lax.div(to, 4), c, lax.rem(to, 4), y)

    def flipped(m, mirror=False):
        to_h = 1 - zh if m & 2 else zh
        to_c = 1 - c if m & 1 else c
        return at(x, to_h, to_c, 3 - zl if mirror and m & 2 else zl, y)

    sibling = flipped(1)

    def block(index, size):
        return pl.ds(pl.multiple_of(index * size, size), size)

    own = [
        pltpu.make_async_copy(basis, basis_g.at[block(y, 512)], own_sem.at[0]),
        pltpu.make_async_copy(acts.at[:, block(zl, 2048)], acts_g.at[0], own_sem.at[1]),
        pltpu.make_async_copy(projection, proj_g.at[0], own_sem.at[2]),
        pltpu.make_async_copy(factor, fac_g.at[0], own_sem.at[3]),
    ]
    for d in range(4):
        own.append(
            pltpu.make_async_copy(
                store.at[off(x, d, 4), zh, c],
                store_g.at[pl.ds(d * 128, 128), block(zh, 256)],
                own_sem.at[4 + d],
            )
        )

    barrier = pltpu.get_barrier_semaphore()
    partners = [along_x(d) for d in range(1, 4)] + [along_y(d) for d in range(1, 4)]
    partners += [along_z(d) for d in range(1, 8)] + [sibling, flipped(3), flipped(3, True)]
    for partner in partners:
        pl.semaphore_signal(barrier, inc=1, device_id=partner, device_id_type=pl.DeviceIdType.MESH)
    for copy in own:
        copy.start()
    for j in range(4):
        rows = 1.0 / (eigvals[j * 16 : j * 16 + 16] + damping)
        for to_c in range(2):
            inv_own[to_c, j] = jnp.concatenate(
                [rows[4 * to_c : 4 * to_c + 4], rows[8 + 4 * to_c : 12 + 4 * to_c]], axis=0
            )
    pl.semaphore_wait(barrier, len(partners))

    mine = block(x * 2 + c, 16)
    line, rings = [], {}
    for h in range(2):
        for d in range(1, 4):
            to = off(zl, d, 4)
            line.append(
                send(
                    acts.at[mine, pl.ds(pl.multiple_of(to * 2048 + h * 1024, 1024), 1024)],
                    acts_g.at[4 - d, mine, pl.ds(h * 1024, 1024)],
                    az_sem, (h, d - 1), at(x, zh, c, to, y),
                )
            )
        if h == 0:
            for n, (half, d) in enumerate(((0, 1), (1, 3), (1, 1), (0, 3))):
                slot = pl.ds(pl.multiple_of(y * 512 + half * 256, 256), 256)
                rings[n] = send(basis.at[pl.ds(half * 256, 256)], basis_g.at[slot], basis_sem, (n,), along_y(d))

    behind = []
    for m in range(1, 4):
        to_c = 1 - c if m & 1 else c
        behind.append(send(inv_own.at[to_c], inv_g.at[m - 1], iv_sem, (m - 1,), flipped(m, True)))
        if m < 3:
            behind.append(send(projection, proj_g.at[m], pr_sem, (m - 1,), flipped(m, True)))
    crossing = behind[3]
    behind.append(send(factor, fac_g.at[1], of_sem, (0,), flipped(2)))

    def offer(m):
        to_h = 1 - zh if m & 2 else zh
        to_c = 1 - c if m & 1 else c
        return [
            send(
                store.at[off(x, d, 4), to_h, to_c],
                store_g.at[pl.ds(d * 128, 128), pl.ds(pl.multiple_of((m & 1) * 512 + zh * 256, 256), 256)],
                st_sem, (m - 1, d), flipped(m),
            )
            for d in range(4)
        ]

    shared, paired = [], []
    for h in range(2):
        for copy in line[3 * h : 3 * h + 3]:
            copy.wait_recv()
        slot = acts_g.at[pl.ds(1, 3), mine, pl.ds(h * 1024, 1024)]
        for dx in (1, 3, 2):
            shared.append((h, dx, send(slot, slot, ax_sem, (h, dx - 1), along_x(dx))))
        paired.append(send(slot, slot, ac_sem, (h, 0), sibling))
    later = offer(2) + offer(1)
    rings[0].wait_recv()
    slot = basis_g.at[pl.ds(pl.multiple_of(off(y, 3, 4) * 512, 256), 256)]
    rings[4] = send(slot, slot, basis_sem, (4,), along_y(1))
    rings[1].wait_recv()
    slot = basis_g.at[pl.ds(pl.multiple_of(off(y, 1, 4) * 512 + 256, 256), 256)]
    rings[5] = send(slot, slot, basis_sem, (5,), along_y(3))
    for h, dx, copy in shared:
        copy.wait_recv()
        slot = acts_g.at[pl.ds(1, 3), block(off(x, 4 - dx, 4) * 2 + c, 16), pl.ds(h * 1024, 1024)]
        paired.append(send(slot, slot, ac_sem, (h, dx), sibling))
    for copy in own[:2]:
        copy.wait()
    for n in range(2, 6):
        rings[n].wait_recv()

    partial = []
    for d in (0, 2, 1, 3):
        if d == 2:
            for copy in paired:
                copy.wait_recv()
        value = jnp.dot(acts_g[d], basis_g[...], preferred_element_type=f32)
        part[d] = value.reshape(2, 64, 512)
        for h in (1, 0):
            if h or d:
                to_h = 1 - zh if h else zh
                partial.append(
                    send(part.at[d, to_h], landed.at[h, d], zr_sem, (h, d), at(x, to_h, c, off(zl, d, 4), y))
                )
    landed[0, 0] = part[0, zh]

    for copy in own[2:]:
        copy.wait()
    crossing.wait_recv()
    behind[2 - 1].wait_recv()
    through = send(proj_g.at[2], proj_g.at[3], pr_sem, (2,), sibling)
    for n, copy in enumerate(behind):
        if n not in (1, 3):
            copy.wait_recv()
    through.wait_recv()
    for m in range(4):
        for k in range(4):
            wide[k * 64 : k * 64 + 64, m * 512 : m * 512 + 512] = proj_g[m]
    spread = (
        lax.div(lax.broadcasted_iota(jnp.int32, (4, 256), 1), 64) == lax.broadcasted_iota(jnp.int32, (4, 256), 0)
    ).astype(f32)
    factors = []
    for h in range(2):
        values = lax.dot_general(
            fac_g[h], spread, (((0,), (0,)), ((), ())),
            preferred_element_type=f32, precision=lax.Precision.HIGHEST,
        )
        factors.append(jnp.where(zh == 0, values[:64], values[64:]))

    for copy in partial:
        copy.wait_recv()
    for h in range(2):
        rotated[0, h] = (landed[h, 0] + landed[h, 1]) + (landed[h, 2] + landed[h, 3])
    across = send(rotated.at[0], rotated.at[1], rc_sem, (0,), sibling)
    later += offer(3)
    across.wait_recv()

    lanes = lax.broadcasted_iota(jnp.int32, (64, 256), 1)
    scattered = []
    for d in (2, 1, 3, 0):
        for h in range(2):
            lefts = []
            for m in range(4):
                source = inv_own.at[c] if m == 0 else inv_g.at[m - 1]
                heights = source[off(x, d, 4)][h * 4 : h * 4 + 4]
                scaled = (rotated[m & 1, m >> 1][None, :, :] * heights[:, None, :]).astype(bf16)
                lefts.append(scaled.reshape(256, 512))
            value = lax.dot_general(
                jnp.concatenate(lefts, axis=1), wide[...], NT, preferred_element_type=f32
            ).reshape(4, 64, 256)
            summed[d, h] = jnp.where(
                lanes < 128,
                jnp.where(lanes < 64, value[0], value[1]),
                jnp.where(lanes < 192, value[2], value[3]),
            )
        if d:
            scattered.append(send(summed.at[d], summed_in.at[d - 1], cx_sem, (d - 1,), along_x(d)))
    for copy in scattered:
        copy.wait_recv()
    for h in range(2):
        total = (summed[0, h] + summed_in[0, h]) + (summed_in[1, h] + summed_in[2, h])
        scale = jnp.where(zh == h, factors[0], factors[1])
        feats[0, 0, :, h * 256 : h * 256 + 256] = (total * scale).astype(bf16)

    def lane(first, count):
        return pl.ds(first * 256, count * 256)

    def slots(level):
        return pl.ds(LEVELS[level][0], len(LEVELS[level]))

    levels, planes, pairs, reduced = {}, {}, {}, {}

    def pair(dy, level):
        pairs[dy, level] = send(
            feats.at[dy, slots(level), :, lane(0, 2)], feats.at[dy, slots(level), :, lane(2, 2)],
            fc_sem, (dy, level), sibling,
        )

    def climb(level):
        if level < 3:
            down = 0 if level == 0 else LEVELS[level][0]
            up = 0 if level == 0 else LEVELS[level][1]
            levels[level + 1] = [
                send(feats.at[0, down, :, lane(0, 2)], feats.at[0, 2 * level + 1, :, lane(0, 2)], fz_sem, (level, 0), along_z(7)),
                send(feats.at[0, up, :, lane(0, 2)], feats.at[0, 2 * level + 2, :, lane(0, 2)], fz_sem, (level, 1), along_z(1)),
            ]
        elif level == 3:
            levels[4] = [
                send(feats.at[0, 5, :, lane(0, 1)], feats.at[0, 7, :, lane(0, 1)], fz_sem, (3, 0), along_z(7)),
                send(feats.at[0, 6, :, lane(1, 1)], feats.at[0, 7, :, lane(1, 1)], fz_sem, (3, 1), along_z(1)),
            ]

    def spread_out(level):
        if level:
            for copy in levels[level]:
                copy.wait_recv()
        climb(level)
        src = feats.at[0, slots(level), :, lane(0, 2)]
        planes[1, level] = send(src, feats.at[3, slots(level), :, lane(0, 2)], fy_sem, (0, level), along_y(1))
        planes[3, level] = send(src, feats.at[1, slots(level), :, lane(0, 2)], fy_sem, (1, level), along_y(3))
        pair(0, level)

    def relay(level):
        planes[1, level].wait_recv()
        planes[2, level] = send(
            feats.at[3, slots(level), :, lane(0, 1)], feats.at[2, slots(level), :, lane(0, 1)],
            fy_sem, (2, level), along_y(1),
        )
        pair(3, level)
        planes[3, level].wait_recv()
        planes[4, level] = send(
            feats.at[1, slots(level), :, lane(1, 1)], feats.at[2, slots(level), :, lane(1, 1)],
            fy_sem, (3, level), along_y(3),
        )
        pair(1, level)

    def relayed(level):
        planes[2, level].wait_recv()
        planes[4, level].wait_recv()
        pair(2, level)

    def place(dy, slot):
        to = off(z, OFFSETS[slot], 8)
        return lax.rem(to, 4), off(y, dy, 4), lax.div(to, 4)

    def score(dy, level):
        pairs[dy, level].wait_recv()
        first, count = LEVELS[level][0], len(LEVELS[level])
        value = lax.dot_general(
            feats[dy, first : first + count].reshape(count * 64, 1024), store_g[...], NT,
            preferred_element_type=f32,
        )
        for n in range(count):
            rows = value[n * 64 : n * 64 + 64]
            for k in range(1, 4):
                going[k - 1, dy, first + n] = rows[:, k * 128 : k * 128 + 128].astype(bf16)
            out[place(dy, first + n)] = rows[:, :128]
        reduced[dy, level] = [
            send(
                going.at[k - 1, dy, slots(level)], coming.at[k - 1, dy, slots(level)],
                sx_sem, (k - 1, dy, level), along_x(k),
            )
            for k in (2, 1, 3)
        ]

    def finish(dy, level):
        for copy in reduced[dy, level]:
            copy.wait_recv()
        for slot in LEVELS[level]:
            rest = coming[0, dy, slot].astype(f32) + coming[1, dy, slot].astype(f32)
            spot = place(dy, slot)
            out[spot] = out[spot] + (rest + coming[2, dy, slot].astype(f32))

    spread_out(0)
    spread_out(1)
    for copy in later:
        copy.wait_recv()
    done = []
    for level in range(5):
        score(0, level)
        if level + 2 < 5:
            spread_out(level + 2)
        relay(level)
        score(3, level)
        score(1, level)
        relayed(level)
        score(2, level)
        if level:
            for dy in (0, 3, 1, 2):
                finish(dy, level - 1)
    for dy in (0, 3, 1, 2):
        finish(dy, 4)
    for copy in sent:
        copy.wait_send()


def body(acts, basis, eigvals, projection, out_factor, store):
    bf16, f32 = jnp.bfloat16, jnp.float32
    sems = [(8,)] + [
        (2, *n)
        for n in [
            (6,), (2, 3), (2, 3), (2, 4), (3, 4), (3,), (3,), (1,), (2, 4), (1,), (3,),
            (4, 2), (4, 5), (4, 5), (3, 4, 5),
        ]
    ]
    vmem = pl.BlockSpec(memory_space=pltpu.VMEM)
    hbm = pl.BlockSpec(memory_space=pl.ANY)
    scores = pl.pallas_call(
        kernel,
        out_shape=jax.ShapeDtypeStruct((4, 4, 2, 64, 128), f32),
        in_specs=[hbm, hbm, vmem, hbm, hbm, hbm],
        out_specs=vmem,
        scratch_shapes=[
            pltpu.VMEM((4, 128, 2048), bf16),
            pltpu.VMEM((2048, 512), bf16),
            pltpu.VMEM((4, 2, 64, 512), f32),
            pltpu.VMEM((2, 4, 64, 512), f32),
            pltpu.VMEM((2, 2, 64, 512), f32),
            pltpu.VMEM((2, 4, 8, 512), f32),
            pltpu.VMEM((3, 4, 8, 512), f32),
            pltpu.VMEM((4, 64, 512), bf16),
            pltpu.VMEM((256, 2048), bf16),
            pltpu.VMEM((2, 4, 128), f32),
            pltpu.VMEM((512, 1024), bf16),
            pltpu.VMEM((4, 2, 64, 256), f32),
            pltpu.VMEM((3, 2, 64, 256), f32),
            pltpu.VMEM((4, 8, 64, 1024), bf16),
            pltpu.VMEM((3, 4, 8, 64, 128), bf16),
            pltpu.VMEM((3, 4, 8, 64, 128), bf16),
        ]
        + [pltpu.SemaphoreType.DMA(n) for n in sems],
        compiler_params=pltpu.CompilerParams(
            collective_id=0, has_side_effects=True, vmem_limit_bytes=60 * 1024 * 1024
        ),
        cost_estimate=pl.CostEstimate(flops=4 * 10**9, bytes_accessed=10**7, transcendentals=0),
    )(acts, basis, eigvals, projection.T, out_factor.T, store.reshape(4, 2, 2, 128, 256))
    return scores.reshape(2048, 128)


def solution(mesh):
    placed = (
        P("store", None),
        P("store", "eig"),
        P(None, "eig"),
        P("eig", None),
        P("store", "eig"),
        P("store", "eig"),
    )
    return jax.shard_map(
        body, mesh=mesh, in_specs=placed, out_specs=P(None, ("store", "eig")), check_vma=False
    )
```

time: 480 us -> 123 us (0.26)
  waiting for transfers between devices: 411 us -> 0 us
  Pallas kernels: 0 us -> 121 us
  blocking collectives: 28.1 us -> 0 us
  matrix products: 17 us -> 0 us
  between operations: 13.2 us -> 0.01 us
  other arithmetic: 5.2 us -> 0 us
    reduce_scatter x2 -> x0, waiting for transfers between devices: 303 us -> none  [the longest x1 221 us: body(): lax.psum_scatter(partial_scores, 'eig', scatter_dimension=1, tiled=True)]
    pallas_call x0 -> x1, Pallas kernels: none -> 121 us  [body(): pl.pallas_call(kernel, out_shape=jax.ShapeDtypeStruct((4, 4, 2, 64, 128),...]
    all_gather x1 -> x0, waiting for transfers between devices: 107 us -> none  [body(): lax.all_gather(basis, 'store', axis=0, tiled=True)]
    all_to_all x1 -> x0, blocking collectives: 28.1 us -> none  [from_everyone(): return lax.all_to_all(copies, axis, split_axis=0, concat_axis=0, tiled=True)]
    dot_general x3 -> x0, matrix products: 17 us -> none  [the longest x1 8.11 us: body(): jnp.einsum('qf,rf->qr', gathered_copies(features, 'store', 0), store, pre...]
    reshape x1 -> x0, local copies, waits for them, and re-layouts: 4.84 us -> none  [body(): partial_value = partial_value.reshape(queries, K_OUT * K_IN)]
  transfers between devices with their start and end apart: 3 -> 0, of which waited for: 3 -> 0; matrix products, arithmetic and copies ran while one was open for 0% -> 0% of each run, Pallas kernels for 0% -> 0%
where the time goes in v2:
time: 123 us
  Pallas kernels  121 us (98%)
  local copies, waits for them, and re-layouts  2.26 us (2%)
    pallas_call x1, Pallas kernels, body(): pl.pallas_call(kernel, out_shape=jax.ShapeDtypeStruct((4, 4, 2, 64, 128),...  121 us

profile of v2, /device:TPU:1, one launch (start us, length us, event | category | flops | bytes accessed | tf_op | source)
XLA Modules:
  0.0 122.8 jit_solution(6153538029923175178)
XLA Ops:
  0.0 120.5 %shard_map.64 = f32[4,4,2,64,128]{4,3,2,1,0:T(8,128)} custom-call(bf16[128,8192]{1,0:T(8,128)(2,1)} %acts.1, bf16[512,512]{1,0:T(8,128)(2,1)} %basis.1, f32[64,512]{1,0:T(8,128)} %eigvals.1, bf16[64,512]{1,0:T(8,128)(2,1)} %bitcast.6, f32[4,128]{1,0:T(4,128)} %bitcast.7, bf16[4,2,2,128,256]{4,3,2,1,0:T(8,128)(2,1)} %bitcast.5), custom_call_target="tpu_custom_call" | custom-call | flops 4000000000 | bytes 10000000 | tf_op jit(solution)/shard_map/pallas_call | solution.py:358
  120.5 2.3 %copy.8 = f32[2048,128]{1,0:T(8,128)} copy(f32[2048,128]{1,0:T(8,128)} %bitcast.4) | data formatting | bytes 2097152

commit v3 on v2

--- a/solution.py
+++ b/solution.py
@@ -165,14 +165,15 @@
             for copy in paired:
                 copy.wait_recv()
         value = jnp.dot(acts_g[d], basis_g[...], preferred_element_type=f32)
-        part[d] = value.reshape(2, 64, 512)
+        part[d] = value.reshape(2, 64, 512).astype(bf16)
+        if d == 0:
+            rotated[0, 0] = jnp.where(zh == 0, value[:64], value[64:])
         for h in (1, 0):
             if h or d:
                 to_h = 1 - zh if h else zh
                 partial.append(
                     send(part.at[d, to_h], landed.at[h, d], zr_sem, (h, d), at(x, to_h, c, off(zl, d, 4), y))
                 )
-    landed[0, 0] = part[0, zh]
 
     for copy in own[2:]:
         copy.wait()
@@ -200,7 +201,9 @@
     for copy in partial:
         copy.wait_recv()
     for h in range(2):
-        rotated[0, h] = (landed[h, 0] + landed[h, 1]) + (landed[h, 2] + landed[h, 3])
+        first = landed[1, 0].astype(f32) if h else rotated[0, 0]
+        rest = landed[h, 2].astype(f32) + landed[h, 3].astype(f32)
+        rotated[0, h] = (first + landed[h, 1].astype(f32)) + rest
     across = send(rotated.at[0], rotated.at[1], rc_sem, (0,), sibling)
     later += offer(3)
     across.wait_recv()
@@ -321,25 +324,23 @@
             spot = place(dy, slot)
             out[spot] = out[spot] + (rest + coming[2, dy, slot].astype(f32))
 
-    spread_out(0)
-    spread_out(1)
-    for copy in later:
-        copy.wait_recv()
-    done = []
-    for level in range(5):
-        score(0, level)
-        if level + 2 < 5:
-            spread_out(level + 2)
-        relay(level)
-        score(3, level)
-        score(1, level)
-        relayed(level)
-        score(2, level)
-        if level:
+    for step in range(9):
+        if step < 5:
+            spread_out(step)
+            if step == 0:
+                for copy in later:
+                    copy.wait_recv()
+            score(0, step)
+        if 0 <= step - 1 < 5:
+            relay(step - 1)
+            score(3, step - 1)
+            score(1, step - 1)
+        if 0 <= step - 2 < 5:
+            relayed(step - 2)
+            score(2, step - 2)
+        if step >= 4:
             for dy in (0, 3, 1, 2):
-                finish(dy, level - 1)
-    for dy in (0, 3, 1, 2):
-        finish(dy, 4)
+                finish(dy, step - 4)
     for copy in sent:
         copy.wait_send()
 
@@ -363,8 +364,8 @@
         scratch_shapes=[
             pltpu.VMEM((4, 128, 2048), bf16),
             pltpu.VMEM((2048, 512), bf16),
-            pltpu.VMEM((4, 2, 64, 512), f32),
-            pltpu.VMEM((2, 4, 64, 512), f32),
+            pltpu.VMEM((4, 2, 64, 512), bf16),
+            pltpu.VMEM((2, 4, 64, 512), bf16),
             pltpu.VMEM((2, 2, 64, 512), f32),
             pltpu.VMEM((2, 4, 8, 512), f32),
             pltpu.VMEM((3, 4, 8, 512), f32),

time: 123 us -> 97.3 us (0.79)
  Pallas kernels: 121 us -> 94.9 us
    pallas_call x1, Pallas kernels: 121 us -> 94.9 us  [body(): pl.pallas_call(kernel, out_shape=jax.ShapeDtypeStruct((4, 4, 2, 64, 128),...]
where the time goes in v3:
time: 97.3 us; the launch traced here: 97.2 us
  Pallas kernels  94.9 us (98%)
  local copies, waits for them, and re-layouts  2.26 us (2%)
    pallas_call x1, Pallas kernels, body(): pl.pallas_call(kernel, out_shape=jax.ShapeDtypeStruct((4, 4, 2, 64, 128),...  94.9 us
    unnamed x1, local copies, waits for them, and re-layouts  2.26 us

profile of v3, /device:TPU:1, one launch (start us, length us, event | category | flops | bytes accessed | tf_op | source)
XLA Modules:
  0.0 97.2 jit_solution(8032521884272297487)
XLA Ops:
  0.0 94.9 %shard_map.64 = f32[4,4,2,64,128]{4,3,2,1,0:T(8,128)} custom-call(bf16[128,8192]{1,0:T(8,128)(2,1)} %acts.1, bf16[512,512]{1,0:T(8,128)(2,1)} %basis.1, f32[64,512]{1,0:T(8,128)} %eigvals.1, bf16[64,512]{1,0:T(8,128)(2,1)} %bitcast.6, f32[4,128]{1,0:T(4,128)} %bitcast.7, bf16[4,2,2,128,256]{4,3,2,1,0:T(8,128)(2,1)} %bitcast.5), custom_call_target="tpu_custom_call" | custom-call | flops 4000000000 | bytes 10000000 | tf_op jit(solution)/shard_map/pallas_call | solution.py:359
  94.9 2.3 %copy.8 = f32[2048,128]{1,0:T(8,128)} copy(f32[2048,128]{1,0:T(8,128)} %bitcast.4) | data formatting | bytes 2097152

commit v4 on v3

--- a/solution.py
+++ b/solution.py
@@ -7,20 +7,22 @@
 
 damping = 0.1
 NT = (((1,), (1,)), ((), ()))
+NN = (((1,), (0,)), ((), ()))
 
 
 def at(x, zh, c, zl, y):
     return {"eig": x * 4 + zh * 2 + c, "store": zl * 4 + y}
 
 
+DIRECT = (0, 4)
 LEVELS = ((0,), (1, 2), (3, 4), (5, 6), (7,))
 OFFSETS = (0, 1, 7, 2, 6, 3, 5, 4)
 
 
 def kernel(
     acts, basis, eigvals, projection, factor, store, out,
-    acts_g, basis_g, part, landed, rotated, inv_own, inv_g, proj_g, wide, fac_g, store_g,
-    summed, summed_in, feats, going, coming,
+    acts_g, basis_g, part, landed, rotated, inv_own, inv_g, proj_g, wide, fac_g, store_g, store_t,
+    halfway, summed, summed_in, feats, going, coming,
     own_sem, basis_sem, az_sem, ax_sem, ac_sem, st_sem, iv_sem, pr_sem, of_sem,
     zr_sem, rc_sem, cx_sem, fz_sem, fy_sem, fc_sem, sx_sem,
 ):
@@ -98,21 +100,23 @@
     pl.semaphore_wait(barrier, len(partners))
 
     mine = block(x * 2 + c, 16)
-    line, rings = [], {}
-    for h in range(2):
-        for d in range(1, 4):
-            to = off(zl, d, 4)
-            line.append(
-                send(
-                    acts.at[mine, pl.ds(pl.multiple_of(to * 2048 + h * 1024, 1024), 1024)],
-                    acts_g.at[4 - d, mine, pl.ds(h * 1024, 1024)],
-                    az_sem, (h, d - 1), at(x, zh, c, to, y),
-                )
-            )
-        if h == 0:
-            for n, (half, d) in enumerate(((0, 1), (1, 3), (1, 1), (0, 3))):
-                slot = pl.ds(pl.multiple_of(y * 512 + half * 256, 256), 256)
-                rings[n] = send(basis.at[pl.ds(half * 256, 256)], basis_g.at[slot], basis_sem, (n,), along_y(d))
+    line, rings = {}, {}
+    for d in (1, 3, 2):
+        to = off(zl, d, 4)
+        line[d] = send(
+            acts.at[mine, block(to, 2048)], acts_g.at[4 - d, mine], az_sem, (d - 1,), at(x, zh, c, to, y)
+        )
+
+    def quarter(at_y, half, j):
+        rows = pl.ds(pl.multiple_of(at_y * 512 + half * 256, 256), 256)
+        return basis_g.at[rows, pl.ds(j * 256, 256)]
+
+    for j in range(2):
+        for n, (half, d) in enumerate(((0, 1), (1, 3), (1, 1), (0, 3))):
+            rings[j, n] = send(
+                basis.at[pl.ds(half * 256, 256), pl.ds(j * 256, 256)], quarter(y, half, j),
+                basis_sem, (j, n), along_y(d),
+            )
 
     behind = []
     for m in range(1, 4):
@@ -135,45 +139,63 @@
             for d in range(4)
         ]
 
-    shared, paired = [], []
-    for h in range(2):
-        for copy in line[3 * h : 3 * h + 3]:
+    shared, paired, partial = {}, {1: [], 2: [], 3: []}, []
+    for d in (1, 3, 2):
+        line[d].wait_recv()
+        slot = acts_g.at[4 - d, mine]
+        shared[d] = [(dx, send(slot, slot, ax_sem, (d - 1, dx - 1), along_x(dx))) for dx in (1, 3, 2)]
+        paired[d].append(send(slot, slot, ac_sem, (d - 1, 0), sibling))
+    later = offer(2) + offer(1)
+
+    def pass_on(j):
+        rings[j, 0].wait_recv()
+        slot = quarter(off(y, 3, 4), 0, j)
+        rings[j, 4] = send(slot, slot, basis_sem, (j, 4), along_y(1))
+        rings[j, 1].wait_recv()
+        slot = quarter(off(y, 1, 4), 1, j)
+        rings[j, 5] = send(slot, slot, basis_sem, (j, 5), along_y(3))
+
+    def share(d):
+        for dx, copy in shared[d]:
             copy.wait_recv()
-        slot = acts_g.at[pl.ds(1, 3), mine, pl.ds(h * 1024, 1024)]
-        for dx in (1, 3, 2):
-            shared.append((h, dx, send(slot, slot, ax_sem, (h, dx - 1), along_x(dx))))
-        paired.append(send(slot, slot, ac_sem, (h, 0), sibling))
-    later = offer(2) + offer(1)
-    rings[0].wait_recv()
-    slot = basis_g.at[pl.ds(pl.multiple_of(off(y, 3, 4) * 512, 256), 256)]
-    rings[4] = send(slot, slot, basis_sem, (4,), along_y(1))
-    rings[1].wait_recv()
-    slot = basis_g.at[pl.ds(pl.multiple_of(off(y, 1, 4) * 512 + 256, 256), 256)]
-    rings[5] = send(slot, slot, basis_sem, (5,), along_y(3))
-    for h, dx, copy in shared:
-        copy.wait_recv()
-        slot = acts_g.at[pl.ds(1, 3), block(off(x, 4 - dx, 4) * 2 + c, 16), pl.ds(h * 1024, 1024)]
-        paired.append(send(slot, slot, ac_sem, (h, dx), sibling))
+            slot = acts_g.at[4 - d, block(off(x, 4 - dx, 4) * 2 + c, 16)]
+            paired[d].append(send(slot, slot, ac_sem, (d - 1, dx), sibling))
+
+    def rotate(d, j):
+        cols = slice(j * 256, j * 256 + 256)
+        value = jnp.dot(acts_g[d], basis_g[:, cols], preferred_element_type=f32)
+        part[d, :, :, cols] = value.reshape(2, 64, 256).astype(bf16)
+        if d == 0:
+            rotated[0, 0, :, cols] = jnp.where(zh == 0, value[:64], value[64:])
+        for h in (1, 0):
+            if h or d:
+                to_h = 1 - zh if h else zh
+                piece = pl.ds(j * 256, 256)
+                partial.append(
+                    send(
+                        part.at[d, to_h, :, piece], landed.at[h, d, :, piece],
+                        zr_sem, (j, h, d), at(x, to_h, c, off(zl, d, 4), y),
+                    )
+                )
+
+    pass_on(0)
+    share(1)
     for copy in own[:2]:
         copy.wait()
     for n in range(2, 6):
-        rings[n].wait_recv()
-
-    partial = []
-    for d in (0, 2, 1, 3):
-        if d == 2:
-            for copy in paired:
-                copy.wait_recv()
-        value = jnp.dot(acts_g[d], basis_g[...], preferred_element_type=f32)
-        part[d] = value.reshape(2, 64, 512).astype(bf16)
-        if d == 0:
-            rotated[0, 0] = jnp.where(zh == 0, value[:64], value[64:])
-        for h in (1, 0):
-            if h or d:
-                to_h = 1 - zh if h else zh
-                partial.append(
-                    send(part.at[d, to_h], landed.at[h, d], zr_sem, (h, d), at(x, to_h, c, off(zl, d, 4), y))
-                )
+        rings[0, n].wait_recv()
+    rotate(0, 0)
+    pass_on(1)
+    for d in (1, 3, 2):
+        if d != 2:
+            share(4 - d if d == 1 else 2)
+        for copy in paired[d]:
+            copy.wait_recv()
+        rotate(4 - d, 0)
+    for n in range(2, 6):
+        rings[1, n].wait_recv()
+    for d in (2, 1, 3, 0):
+        rotate(d, 1)
 
     for copy in own[2:]:
         copy.wait()
@@ -184,9 +206,9 @@
         if n not in (1, 3):
             copy.wait_recv()
     through.wait_recv()
-    for m in range(4):
+    for n, m in enumerate((0, 2, 1, 3)):
         for k in range(4):
-            wide[k * 64 : k * 64 + 64, m * 512 : m * 512 + 512] = proj_g[m]
+            wide[k * 64 : k * 64 + 64, n * 512 : n * 512 + 512] = proj_g[m]
     spread = (
         lax.div(lax.broadcasted_iota(jnp.int32, (4, 256), 1), 64) == lax.broadcasted_iota(jnp.int32, (4, 256), 0)
     ).astype(f32)
@@ -198,6 +220,16 @@
         )
         factors.append(jnp.where(zh == 0, values[:64], values[64:]))
 
+    def turn_over(m):
+        at_h = 1 - zh if m & 2 else zh
+        place_of = pl.ds(pl.multiple_of((m & 1) * 512 + at_h * 256, 256), 256)
+        store_t[place_of] = store_g[:, place_of].T
+
+    for copy in later:
+        copy.wait_recv()
+    for m in range(3):
+        turn_over(m)
+
     for copy in partial:
         copy.wait_recv()
     for h in range(2):
@@ -205,22 +237,29 @@
         rest = landed[h, 2].astype(f32) + landed[h, 3].astype(f32)
         rotated[0, h] = (first + landed[h, 1].astype(f32)) + rest
     across = send(rotated.at[0], rotated.at[1], rc_sem, (0,), sibling)
-    later += offer(3)
+    last = offer(3)
+
+    def project(d, h, core):
+        lefts = []
+        for m in (core, core + 2):
+            source = inv_own.at[c] if m == 0 else inv_g.at[m - 1]
+            heights = source[off(x, d, 4)][h * 4 : h * 4 + 4]
+            scaled = (rotated[core, m >> 1][None, :, :] * heights[:, None, :]).astype(bf16)
+            lefts.append(scaled.reshape(256, 512))
+        return lax.dot_general(
+            jnp.concatenate(lefts, axis=1), wide[:, core * 1024 : core * 1024 + 1024], NT,
+            preferred_element_type=f32,
+        )
+
+    for d in (2, 1, 3, 0):
+        for h in range(2):
+            halfway[d, h] = project(d, h, 0)
     across.wait_recv()
-
     lanes = lax.broadcasted_iota(jnp.int32, (64, 256), 1)
     scattered = []
     for d in (2, 1, 3, 0):
         for h in range(2):
-            lefts = []
-            for m in range(4):
-                source = inv_own.at[c] if m == 0 else inv_g.at[m - 1]
-                heights = source[off(x, d, 4)][h * 4 : h * 4 + 4]
-                scaled = (rotated[m & 1, m >> 1][None, :, :] * heights[:, None, :]).astype(bf16)
-                lefts.append(scaled.reshape(256, 512))
-            value = lax.dot_general(
-                jnp.concatenate(lefts, axis=1), wide[...], NT, preferred_element_type=f32
-            ).reshape(4, 64, 256)
+            value = (halfway[d, h] + project(d, h, 1)).reshape(4, 64, 256)
             summed[d, h] = jnp.where(
                 lanes < 128,
                 jnp.where(lanes < 64, value[0], value[1]),
@@ -269,27 +308,33 @@
                 copy.wait_recv()
         climb(level)
         src = feats.at[0, slots(level), :, lane(0, 2)]
+        if level in DIRECT:
+            far = feats.at[2, slots(level), :, lane(0, 2)]
+            planes[2, level] = send(src, far, fy_sem, (2, level), along_y(2))
         planes[1, level] = send(src, feats.at[3, slots(level), :, lane(0, 2)], fy_sem, (0, level), along_y(1))
         planes[3, level] = send(src, feats.at[1, slots(level), :, lane(0, 2)], fy_sem, (1, level), along_y(3))
         pair(0, level)
 
     def relay(level):
         planes[1, level].wait_recv()
-        planes[2, level] = send(
-            feats.at[3, slots(level), :, lane(0, 1)], feats.at[2, slots(level), :, lane(0, 1)],
-            fy_sem, (2, level), along_y(1),
-        )
+        if level not in DIRECT:
+            planes[2, level] = send(
+                feats.at[3, slots(level), :, lane(0, 1)], feats.at[2, slots(level), :, lane(0, 1)],
+                fy_sem, (2, level), along_y(1),
+            )
         pair(3, level)
         planes[3, level].wait_recv()
-        planes[4, level] = send(
-            feats.at[1, slots(level), :, lane(1, 1)], feats.at[2, slots(level), :, lane(1, 1)],
-            fy_sem, (3, level), along_y(3),
-        )
+        if level not in DIRECT:
+            planes[4, level] = send(
+                feats.at[1, slots(level), :, lane(1, 1)], feats.at[2, slots(level), :, lane(1, 1)],
+                fy_sem, (3, level), along_y(3),
+            )
         pair(1, level)
 
     def relayed(level):
         planes[2, level].wait_recv()
-        planes[4, level].wait_recv()
+        if level not in DIRECT:
+            planes[4, level].wait_recv()
         pair(2, level)
 
     def place(dy, slot):
@@ -300,8 +345,8 @@
         pairs[dy, level].wait_recv()
         first, count = LEVELS[level][0], len(LEVELS[level])
         value = lax.dot_general(
-            feats[dy, first : first + count].reshape(count * 64, 1024), store_g[...], NT,
-            preferred_element_type=f32,
+            feats[dy, first : first + count].reshape(count * 64, 1024), store_t[...],
+            NN, preferred_element_type=f32,
         )
         for n in range(count):
             rows = value[n * 64 : n * 64 + 64]
@@ -327,12 +372,15 @@
     for step in range(9):
         if step < 5:
             spread_out(step)
-            if step == 0:
-                for copy in later:
-                    copy.wait_recv()
+        if step == 0:
+            for copy in last:
+                copy.wait_recv()
+            turn_over(3)
+        if 0 <= step - 1 < 5:
+            relay(step - 1)
+        if step < 5:
             score(0, step)
         if 0 <= step - 1 < 5:
-            relay(step - 1)
             score(3, step - 1)
             score(1, step - 1)
         if 0 <= step - 2 < 5:
@@ -350,7 +398,7 @@
     sems = [(8,)] + [
         (2, *n)
         for n in [
-            (6,), (2, 3), (2, 3), (2, 4), (3, 4), (3,), (3,), (1,), (2, 4), (1,), (3,),
+            (2, 6), (3,), (3, 3), (3, 4), (3, 4), (3,), (3,), (1,), (2, 2, 4), (1,), (3,),
             (4, 2), (4, 5), (4, 5), (3, 4, 5),
         ]
     ]
@@ -373,6 +421,8 @@
             pltpu.VMEM((256, 2048), bf16),
             pltpu.VMEM((2, 4, 128), f32),
             pltpu.VMEM((512, 1024), bf16),
+            pltpu.VMEM((1024, 512), bf16),
+            pltpu.VMEM((4, 2, 256, 256), f32),
             pltpu.VMEM((4, 2, 64, 256), f32),
             pltpu.VMEM((3, 2, 64, 256), f32),
             pltpu.VMEM((4, 8, 64, 1024), bf16),

time: 97.3 us -> 95.8 us (0.985)
  Pallas kernels: 94.9 us -> 93.4 us
    pallas_call x1, Pallas kernels: 94.9 us -> 93.4 us  [body(): pl.pallas_call(kernel, out_shape=jax.ShapeDtypeStruct((4, 4, 2, 64, 128),...]
where the time goes in v4:
time: 95.8 us; the launch traced here: 95.7 us
  Pallas kernels  93.4 us (97%)
  local copies, waits for them, and re-layouts  2.26 us (2%)
    pallas_call x1, Pallas kernels, body(): pl.pallas_call(kernel, out_shape=jax.ShapeDtypeStruct((4, 4, 2, 64, 128),...  93.4 us
    unnamed x1, local copies, waits for them, and re-layouts  2.26 us

profile of v4, /device:TPU:1, one launch (start us, length us, event | category | flops | bytes accessed | tf_op | source)
XLA Modules:
  0.0 95.7 jit_solution(10036021273165286719)
XLA Ops:
  0.0 93.4 %shard_map.64 = f32[4,4,2,64,128]{4,3,2,1,0:T(8,128)} custom-call(bf16[128,8192]{1,0:T(8,128)(2,1)} %acts.1, bf16[512,512]{1,0:T(8,128)(2,1)} %basis.1, f32[64,512]{1,0:T(8,128)} %eigvals.1, bf16[64,512]{1,0:T(8,128)(2,1)} %bitcast.6, f32[4,128]{1,0:T(4,128)} %bitcast.7, bf16[4,2,2,128,256]{4,3,2,1,0:T(8,128)(2,1)} %bitcast.5), custom_call_target="tpu_custom_call" | custom-call | flops 4000000000 | bytes 10000000 | tf_op jit(solution)/shard_map/pallas_call | solution.py:407
  93.4 2.3 %copy.8 = f32[2048,128]{1,0:T(8,128)} copy(f32[2048,128]{1,0:T(8,128)} %bitcast.4) | data formatting | bytes 2097152
